TPU v7x, 32 devices: a whole 2x2x4 slice. The times are simulated.
32 devices in a mesh: dp: 8 (over z, y), row: 2 (over core), col: 2 (over x).
Axes of the slice: x: 2, y: 2, z: 4, core: 2. Of those that a mesh axis runs over, the one named last changes fastest.
Arguments:
- block_input: bfloat16 [4096, 2560], P(('dp', 'col')), may hold values from -6 to 6
- cotangent: bfloat16 [4096, 2560], P(('dp', 'col'), 'row'), may hold values from -6 to 6
- seq_lengths: int32 [32], replicated, may hold values from 16 to 128, as said below
- seq_owner: int32 [32], replicated, may hold values from 0 to 15, as said below
- norm_gain: bfloat16 [2560], P('row'), may hold values from 0.5 to 1.5
- proj_zx: bfloat16 [2560, 2, 5120], P('row', None, 'col'), may hold values from -0.125 to 0.125
- proj_bc: bfloat16 [2560, 256], P('row'), may hold values from -0.125 to 0.125
- proj_dt: bfloat16 [2560, 80], P('row', 'col'), may hold values from -0.125 to 0.125
- proj_out: bfloat16 [5120, 2560], P('col', 'row'), may hold values from -0.078125 to 0.078125
- inner_kernel: float32 [4, 5120], P(None, 'col'), may hold values from -3 to 3
- inner_offset: float32 [5120], P('col'), may hold values from -1.5 to 1.5
- shared_kernel: float32 [4, 256], replicated, may hold values from -3 to 3
- shared_offset: float32 [256], replicated, may hold values from -1.5 to 1.5
- decay_log: float32 [80], P('col'), may hold values from 0 to 2.77
- step_bias: float32 [80], P('col'), may hold values from -6 to -2
- skip_gain: float32 [80], P('col'), may hold values from 0.5 to 1.5
- output_gain: bfloat16 [5120], P('col'), may hold values from 0.5 to 1.5
Outputs:
- block_output: bfloat16 [4096, 2560], P(('dp', 'col'), 'row')
- input_grad: float32 [4096, 2560], P(('dp', 'col'), 'row')
- grad_norm: float32 [2560], P('row')
- grad_inproj: float32 [2560, 2, 5120], P('row', None, 'col')
- grad_shared: float32 [2560, 256], P('row')
- grad_steps: float32 [2560, 80], P('row', 'col')
- grad_outproj: float32 [5120, 2560], P('col', 'row')
- grad_kernel: float32 [4, 5120], P(None, 'col')
- grad_offset: float32 [5120], P('col')
- grad_skernel: float32 [4, 256], replicated
- grad_soffset: float32 [256], replicated
- grad_decay: float32 [80], P('col')
- grad_stepbias: float32 [80], P('col')
- grad_skip: float32 [80], P('col')
- grad_ogain: float32 [5120], P('col')
Inputs may be any that keep to these rules, and one draw needn't show every extreme that they name: `seq_lengths`: the lengths of the 2 sequences of one bucket sum to at most 256; in every draw some bucket holds 2 sequences of exactly 128 rows, so that its sum is 256. `seq_owner`: every bucket owns exactly 2 sequences.
All inputs are finite; a program needn't handle non-finite values.
Results may differ from a plain program's by a relative error of at most 0.0079.
The roundings to bfloat16 on the way count: a program that leaves them out, or rounds other values in their place, can miss the bound.
Values may be sent and summed in bfloat16 or wider, within the bound.
A program may use at most 256 MiB of HBM per device.

v0:
```python
import jax
import jax.numpy as jnp
from jax import lax
from jax.sharding import PartitionSpec as P

D = 2560
DI = 5120
CAP = 256
EPSILON = 1e-05
PRECISE = lax.Precision.HIGHEST


def layout(seq_lengths, seq_owner, bucket, capacity):
    owned = seq_owner == bucket
    owned_len = jnp.where(owned, seq_lengths, 0)
    order = jnp.arange(seq_lengths.shape[0], dtype=jnp.int32)
    starts = jnp.sum(jnp.where(order[None, :] < order[:, None], owned_len[None, :], 0), axis=1)
    places = jnp.arange(capacity, dtype=jnp.int32)[:, None]
    ends = starts + seq_lengths
    inside = owned[None, :] & (places >= starts[None, :]) & (places < ends[None, :])
    live_rows = jnp.any(inside, axis=1)
    seq_index = jnp.arange(seq_lengths.shape[0], dtype=jnp.int32)
    seq_ids = jnp.sum(jnp.where(inside, seq_index[None, :], 0), axis=1)
    seq_ids = jnp.where(live_rows, seq_ids, -1)
    return (seq_ids, live_rows.astype(jnp.float32))


def convolve(channels, kernel, offset, seq_ids, live_rows):
    tap_count = kernel.shape[0]
    summed_in = offset[None, :] + kernel[tap_count - 1][None, :] * channels
    for lag_steps in range(1, tap_count):
        lagged = jnp.concatenate(
            [jnp.zeros((lag_steps, channels.shape[1]), jnp.float32), channels[:-lag_steps]], axis=0
        )
        prior_ids = jnp.concatenate([jnp.full((lag_steps,), -1, jnp.int32), seq_ids[:-lag_steps]])
        same_seq = jnp.where((prior_ids == seq_ids) & (live_rows > 0), 1.0, 0.0).astype(jnp.float32)
        summed_in = (
            summed_in + kernel[tap_count - 1 - lag_steps][None, :] * lagged * same_seq[:, None]
        )
    return summed_in


def mix_bucket(values, bmat, cmat, sizes, rates, skip_gain, ids, live):
    rows_all, head_count, head_dim = values.shape
    lower = jnp.arange(rows_all)[:, None] >= jnp.arange(rows_all)[None, :]
    cumulated = jnp.dot(lower.astype(jnp.float32), rates, precision=PRECISE)
    pair_live = (ids[:, None] == ids[None, :]) & (live[:, None] > 0) & (live[None, :] > 0) & lower
    scores = jnp.dot(cmat, bmat.T, precision=PRECISE)
    gap = jnp.where(pair_live[:, :, None], cumulated[:, None, :] - cumulated[None, :, :], 0.0)
    weights = (
        jnp.exp(gap) * (pair_live.astype(jnp.float32) * scores)[:, :, None] * sizes[None, :, :]
    )
    within = jnp.einsum("tsh,shp->thp", weights, values, precision=PRECISE)
    mixed_out = (within + skip_gain[None, :, None] * values) * live[:, None, None]
    return mixed_out.reshape(rows_all, head_count * head_dim)


def sum_rows_over_dp(part, shared_cols=0):
    piece = lax.psum_scatter(part.astype(jnp.bfloat16), "dp", scatter_dimension=0, tiled=True)
    if shared_cols:
        own = piece.shape[1] - shared_cols
        tail = lax.psum(piece[:, own:].astype(jnp.float32), "col").astype(jnp.bfloat16)
        piece = jnp.concatenate([piece[:, :own], tail], axis=1)
    return lax.all_gather(piece, "dp", axis=0, tiled=True)


def mixer_local(
    conv_in,
    narrow_in,
    inner_kernel,
    inner_offset,
    shared_kernel,
    shared_offset,
    decay_log,
    step_bias,
    skip_gain,
    seq_ids,
    live_rows,
):
    inner_size = inner_kernel.shape[1]
    state_size = shared_kernel.shape[1] // 2
    head_count = decay_log.shape[0]
    shared_in = narrow_in[:, : 2 * state_size]
    step_raw = narrow_in[:, 2 * state_size :]
    mixed_x = jax.nn.silu(convolve(conv_in, inner_kernel, inner_offset, seq_ids, live_rows))
    mixed_bc = jax.nn.silu(convolve(shared_in, shared_kernel, shared_offset, seq_ids, live_rows))
    step_sizes = jax.nn.softplus(step_raw + step_bias[None, :])
    decay_rate = step_sizes * (-jnp.exp(decay_log))[None, :]
    values = mixed_x.reshape(mixed_x.shape[0], head_count, inner_size // head_count)
    return mix_bucket(
        values,
        mixed_bc[:, :state_size],
        mixed_bc[:, state_size:],
        step_sizes,
        decay_rate,
        skip_gain,
        seq_ids,
        live_rows,
    )


def per_device(
    block_input,
    cotangent,
    seq_lengths,
    seq_owner,
    norm_gain,
    proj_zx,
    proj_bc,
    proj_dt,
    proj_out,
    inner_kernel,
    inner_offset,
    shared_kernel,
    shared_offset,
    decay_log,
    step_bias,
    skip_gain,
    output_gain,
):
    row_count = lax.axis_size("row")
    col_count = lax.axis_size("col")
    row_index = lax.axis_index("row")
    col_index = lax.axis_index("col")
    data_index = lax.axis_index("dp")
    width_part = norm_gain.shape[0]
    inner_size = proj_zx.shape[2]
    state_size = proj_bc.shape[1] // 2
    tap_count = inner_kernel.shape[0]
    capacity = CAP
    bucket = data_index * row_count + row_index
    seq_ids, live_rows = layout(seq_lengths, seq_owner, bucket, capacity)
    rscale = lax.rsqrt(
        jnp.mean(jnp.square(block_input.astype(jnp.float32)), axis=1, keepdims=True) + EPSILON
    )
    own_cols = lax.dynamic_slice_in_dim(block_input, row_index * width_part, width_part, 1).astype(
        jnp.float32
    )
    normalized = own_cols * rscale
    gain_f = norm_gain.astype(jnp.float32)
    normed = (normalized * gain_f[None, :]).astype(jnp.bfloat16)
    normed_all = lax.all_gather(normed, "col", axis=0, tiled=True)
    weight_zx = proj_zx.reshape(width_part, 2 * inner_size)
    weight_narrow = jnp.concatenate([proj_bc, proj_dt], axis=1)
    zx_in = lax.psum_scatter(
        jnp.dot(normed_all, weight_zx, preferred_element_type=jnp.float32),
        "row",
        scatter_dimension=0,
        tiled=True,
    )
    narrow_in = lax.psum_scatter(
        jnp.dot(normed_all, weight_narrow, preferred_element_type=jnp.float32),
        "row",
        scatter_dimension=0,
        tiled=True,
    )
    gate_in = zx_in[:, :inner_size]
    conv_in = zx_in[:, inner_size:]

    def local_piece(*operands):
        return mixer_local(*operands, seq_ids, live_rows)

    ssm_rows, pull_back = jax.vjp(
        local_piece,
        conv_in,
        narrow_in,
        inner_kernel,
        inner_offset,
        shared_kernel,
        shared_offset,
        decay_log,
        step_bias,
        skip_gain,
    )
    gated_rows, gate_back = jax.vjp(
        lambda ssm_value, gate_value: ssm_value * jax.nn.silu(gate_value), ssm_rows, gate_in
    )
    square_sum = lax.psum(jnp.sum(gated_rows * gated_rows, axis=1), "col")
    rnorm = lax.rsqrt(square_sum / DI + EPSILON)[:, None]
    out_gain = output_gain.astype(jnp.float32)
    branch = (gated_rows * rnorm * out_gain[None, :]).astype(jnp.bfloat16)
    branch_all = lax.all_gather(branch, "row", axis=0, tiled=True)
    row_piece = branch_all
    branch_out = lax.psum_scatter(
        jnp.dot(row_piece, proj_out, preferred_element_type=jnp.float32),
        "col",
        scatter_dimension=0,
        tiled=True,
    )
    block_output = (own_cols + branch_out).astype(jnp.bfloat16)
    cot_all = lax.all_gather(cotangent, "col", axis=0, tiled=True)
    row_piece = cot_all
    branch_grad = lax.psum_scatter(
        lax.dot_general(
            row_piece, proj_out, (((1,), (1,)), ((), ())), preferred_element_type=jnp.float32
        ),
        "row",
        scatter_dimension=0,
        tiled=True,
    )
    outproj_part = lax.dot_general(
        branch_all, cot_all, (((0,), (0,)), ((), ())), preferred_element_type=jnp.float32
    )
    outproj_total = sum_rows_over_dp(outproj_part).astype(jnp.float32)
    scaled_grad = branch_grad * out_gain[None, :]
    cross_sum = lax.psum(jnp.sum(scaled_grad * gated_rows, axis=1), "col")
    gated_grad = rnorm * scaled_grad - gated_rows * rnorm**3 * (cross_sum / DI)[:, None]
    ogain_part = jnp.sum(branch_grad * gated_rows * rnorm, axis=0)
    ssm_grad, gate_grad = gate_back(gated_grad)
    gate_all = lax.all_gather(gate_grad.astype(jnp.bfloat16), "row", axis=0, tiled=True)
    gate_total = sum_rows_over_dp(
        lax.dot_general(
            normed_all, gate_all, (((0,), (0,)), ((), ())), preferred_element_type=jnp.float32
        )
    )
    local_grads = pull_back(ssm_grad)
    inner_all = lax.all_gather(local_grads[0].astype(jnp.bfloat16), "row", axis=0, tiled=True)
    narrow_all = lax.all_gather(local_grads[1].astype(jnp.bfloat16), "row", axis=0, tiled=True)
    normed_grad = lax.psum_scatter(
        lax.dot_general(
            jnp.concatenate([gate_all, inner_all], axis=1),
            weight_zx,
            (((1,), (1,)), ((), ())),
            preferred_element_type=jnp.float32,
        )
        + lax.dot_general(
            narrow_all, weight_narrow, (((1,), (1,)), ((), ())), preferred_element_type=jnp.float32
        ),
        "col",
        scatter_dimension=0,
        tiled=True,
    )
    inner_total = sum_rows_over_dp(
        lax.dot_general(
            normed_all, inner_all, (((0,), (0,)), ((), ())), preferred_element_type=jnp.float32
        )
    )
    narrow_part = lax.dot_general(
        normed_all, narrow_all, (((0,), (0,)), ((), ())), preferred_element_type=jnp.float32
    )
    narrow_total = sum_rows_over_dp(
        jnp.concatenate([narrow_part[:, 2 * state_size :], narrow_part[:, : 2 * state_size]], 1),
        2 * state_size,
    ).astype(jnp.float32)
    head_count = decay_log.shape[0]
    steps_total = narrow_total[:, :head_count]
    shared_total = narrow_total[:, head_count:]
    inproj_total = jnp.stack([gate_total, inner_total], axis=1).astype(jnp.float32)
    scaled_in = normed_grad * gain_f[None, :]
    norm_part = jnp.sum(normed_grad * normalized, axis=0)
    row_stat = lax.psum(jnp.sum(scaled_in * normalized, axis=1), "row")
    input_grad = cotangent.astype(jnp.float32) + rscale * (
        scaled_in - normalized * (row_stat / D)[:, None]
    )
    row_hot = (jnp.arange(row_count) == row_index).astype(jnp.float32)
    col_hot = (jnp.arange(col_count) == col_index).astype(jnp.float32)
    gain_slot = row_hot[:, None] * norm_part[None, :]
    head_stack = jnp.stack([local_grads[6], local_grads[7], local_grads[8]], axis=0)
    head_slot = col_hot[None, :, None] * head_stack[:, None, :]
    chan_stack = jnp.concatenate(
        [local_grads[2], local_grads[3][None, :], ogain_part[None, :]], axis=0
    )
    chan_slot = col_hot[None, :, None] * chan_stack[:, None, :]
    shared_stack = jnp.concatenate([local_grads[4], local_grads[5][None, :]], axis=0)
    summed = lax.psum((gain_slot, head_slot, chan_slot, shared_stack), ("dp", "row", "col"))
    gain_total = lax.dynamic_index_in_dim(summed[0], row_index, 0, keepdims=False)
    head_total = lax.dynamic_index_in_dim(summed[1], col_index, 1, keepdims=False)
    chan_total = lax.dynamic_index_in_dim(summed[2], col_index, 1, keepdims=False)
    stack_total = summed[3]
    return (
        block_output,
        input_grad,
        gain_total,
        inproj_total,
        shared_total,
        steps_total,
        outproj_total,
        chan_total[:tap_count],
        chan_total[tap_count],
        stack_total[:tap_count],
        stack_total[tap_count],
        head_total[0],
        head_total[1],
        head_total[2],
        chan_total[tap_count + 1],
    )


def solution(mesh):
    return jax.shard_map(
        per_device,
        mesh=mesh,
        in_specs=(
            P(("dp", "col"), None),
            P(("dp", "col"), "row"),
            P(),
            P(),
            P("row"),
            P("row", None, "col"),
            P("row", None),
            P("row", "col"),
            P("col", "row"),
            P(None, "col"),
            P("col"),
            P(),
            P(),
            P("col"),
            P("col"),
            P("col"),
            P("col"),
        ),
        out_specs=(
            P(("dp", "col"), "row"),
            P(("dp", "col"), "row"),
            P("row"),
            P("row", None, "col"),
            P("row", None),
            P("row", "col"),
            P("col", "row"),
            P(None, "col"),
            P("col"),
            P(),
            P(),
            P("col"),
            P("col"),
            P("col"),
            P("col"),
        ),
        check_vma=False,
    )
```

profile of v0, /device:TPU:0, one launch (start us, length us, event | category | flops | bytes accessed | tf_op | source)
XLA Modules:
  0.0 1226.2 jit_solution(14746132511163028913)
XLA Ops:
  9.6 2.1 fusion.48
  12.6 12.3 %copy.74 = bf16[160,8,2,2560]{3,1,2,0:T(8,128)(2,1)} copy(bf16[160,8,2,2560]{3,2,1,0:T(2,128)(2,1)} %bitcast.83) | data formatting | bytes 26214400
  25.1 13.7 %all-gather.9.cloned.1.call-done = bf16[512,1280]{1,0:T(8,128)(2,1)} async-done(((bf16[256,1280]{1,0:T(8,128)(2,1)}), bf16[512,1280]{1,0:T(8,128)(2,1)}) %all-gather.9.cloned.1.call-update) | async-done | bytes 1310736 | tf_op jit(solution)/shard_map/all_gather | solution.py:142
  38.9 2.8 fusion.58
  41.8 12.3 %fusion.106 = f32[512,5120]{1,0:T(8,128)} fusion(bf16[512,1280]{1,0:T(8,128)(2,1)S(1)} %copy-done.17, bf16[1280,5120]{1,0:T(8,128)(2,1)} %bitcast.84), kind=kOutput, calls=%fused_computation.194 | convolution fusion | flops 6710886400 | bytes 24903680 | tf_op jit(solution)/shard_map/dot_general | solution.py:146
  54.2 10.5 all-gather.13.cloned.1.call-done
  64.7 9.2 fusion.108
  79.9 2.1 fusion.62
  83.8 14.8 %reduce-scatter.12.cloned.1.call-done = f32[256,5120]{1,0:T(8,128)} async-done(((f32[512,5120]{1,0:T(8,128)}), f32[256,5120]{1,0:T(8,128)}) %reduce-scatter.12.cloned.1.call-update) | async-done | bytes 5242896 | tf_op jit(solution)/shard_map/reduce_scatter | solution.py:145
  104.2 3.8 fusion.35
  108.0 2.1 copy.60
  110.1 15.6 %fusion.33 = f32[256,40,64]{0,2,1:T(8,128)} fusion(f32[256,40,64]{0,2,1:T(8,128)} %bitcast.88, f32[256,40]{0,1:T(8,128)S(1)} %compare_select_fusion.2, f32[256,256]{1,0:T(8,128)} %convolution_select_fusion, f32[256,40]{0,1:T(8,128)S(1)} %fusion.64, pred[256,256]{1,0:T(8,128)(4,1)S(1)} %fusion.65, f32[256]{0:T(256)S(1)} %get-tuple-element.145, ...), kind=kOutput, calls=%fused_computation.49 | convolution fusion | flops 2025717760 | bytes 5653664 | tf_op jit(solution)/shard_map/jvp(tsh,shp->thp)/dot_general | solution.py:53
  125.7 2.1 copy.62
  127.9 4.0 multiply_reduce_fusion.8
  131.9 4.9 psum.56
  136.8 3.3 multiply_reduce_fusion.2
  140.1 5.2 psum.57
  145.3 6.7 multiply_reduce_fusion.1
  152.0 2.1 copy.64
  154.2 11.6 bitcast_add_fusion
  165.8 3.4 copy.65
  169.2 4.0 multiply_reduce_fusion.6
  177.8 3.2 multiply_reduce_fusion.3
  182.7 18.6 %fusion.8 = (f32[256,40]{0,1:T(8,128)}, f32[256,40]{0,1:T(8,128)}, f32[256,40]{0,1:T(8,128)}, f32[256,256]{1,0:T(8,128)S(1)}) fusion(f32[256,40]{0,1:T(8,128)} %copy-done.31, f32[256,256]{1,0:T(8,128)} %convolution_select_fusion, f32[256,40]{0,1:T(8,128)} %copy-done.66, pred[256,256]{1,0:T(8,128)(4,1)S(1)} %fusion.65, f32[256,40,64]{0,2,1:T(8,128)S(1)} %bitcast.89, ...), kind=kOutput, calls=%fused_computation.15 | convolution fusion | flops 2047903744 | bytes 6038528 | tf_op jit(solution)/shard_map/transpose(jvp(tsh,shp->thp))/dot_general | solution.py:53
  206.3 2.2 all_gather.35
  210.6 7.3 convolution_convert_fusion.1
  218.0 7.6 convolution_convert_fusion.2
  226.9 8.0 convolution_convert_fusion
  236.7 55.0 %reduce-scatter.28.cloned.1.call-done = bf16[160,296]{1,0:T(8,128)(2,1)} async-done(((bf16[1280,296]{1,0:T(8,128)(2,1)}), bf16[160,296]{1,0:T(8,128)(2,1)}) %reduce-scatter.28.cloned.1.call-update) | async-done | bytes 94736
  293.5 13.9 %fusion.9 = f32[512,1280]{1,0:T(8,128)} fusion(bf16[1280,5120]{1,0:T(8,128)(2,1)} %bitcast.85, bf16[512,2560]{1,0:T(8,128)(2,1)} %all-gather.17.cloned.1.call-done, bf16[512,2560]{1,0:T(8,128)(2,1)} %all-gather.15.cloned.1.call-done), kind=kOutput, calls=%fused_computation.16 | convolution fusion | flops 6721372160 | bytes 20971520 | tf_op jit(solution)/shard_map/dot_general | solution.py:220
  307.4 4.1 convolution_add_fusion
  313.2 7.9 fusion.107
  321.2 95.2 %reduce-scatter.24.cloned.1.call-done = bf16[160,2560]{1,0:T(8,128)(2,1)} async-done(((bf16[1280,2560]{1,0:T(8,128)(2,1)}), bf16[160,2560]{1,0:T(8,128)(2,1)}) %reduce-scatter.24.cloned.1.call-update) | async-done | bytes 819216 | tf_op jit(solution)/shard_map/reduce_scatter | solution.py:59
  416.4 124.8 %reduce-scatter.22.cloned.1.call-done = bf16[160,2560]{1,0:T(8,128)(2,1)} async-done(((bf16[1280,2560]{1,0:T(8,128)(2,1)}), bf16[160,2560]{1,0:T(8,128)(2,1)}) %reduce-scatter.22.cloned.1.call-update) | async-done | bytes 819216 | tf_op jit(solution)/shard_map/reduce_scatter | solution.py:59
  541.3 124.2 %reduce-scatter.26.cloned.1.call-done = bf16[320,1280]{1,0:T(8,128)(2,1)} async-done(((bf16[2560,1280]{1,0:T(8,128)(2,1)}), bf16[320,1280]{1,0:T(8,128)(2,1)}) %reduce-scatter.26.cloned.1.call-update) | async-done | bytes 819216 | tf_op jit(solution)/shard_map/reduce_scatter | solution.py:59
  665.9 127.6 %all-reduce.32.cloned.1.call-done = f32[6,2,2560]{2,0,1:T(8,128)} async-done(((f32[6,2,2560]{2,0,1:T(8,128)}), f32[6,2,2560]{2,0,1:T(8,128)}) %all-reduce.32.cloned.1.call-update) | async-done | bytes 122896 | tf_op jit(solution)/shard_map/psum | solution.py:265
  796.7 23.0 %all-reduce.30.cloned.1.call-done = bf16[160,256]{0,1:T(8,128)(2,1)} async-done(((bf16[160,256]{0,1:T(8,128)(2,1)}), bf16[160,256]{0,1:T(8,128)(2,1)}) %all-reduce.30.cloned.1.call-update) | async-done | bytes 81936 | tf_op jit(solution)/shard_map/psum | solution.py:62
  820.8 33.0 %all_gather.38 = bf16[1280,296]{1,0:T(8,128)(2,1)S(1)} all-gather(bf16[160,296]{1,0:T(8,128)(2,1)S(1)} %copy.67), channel_id=1, replica_groups=mesh['dp'=8,'row'=2,'col'=2] {'dp'}, dimensions={0}, use_global_device_ids=true | all-gather | bytes 852480 | tf_op jit(solution)/shard_map/all_gather | solution.py:64
  856.0 4.1 reduce-scatter.20.cloned.1.call-done
  862.1 40.3 %all-reduce.26 = (f32[2,1280]{1,0:T(2,128)S(1)}, f32[5,256]{1,0:T(8,128)S(1)}, f32[3,2,40]{2,1,0:T(2,128)S(1)}) all-reduce(f32[2,1280]{1,0:T(2,128)S(1)} %broadcast_multiply_fusion.7, f32[5,256]{1,0:T(8,128)S(1)} %pad_maximum_fusion.6, ...), channel_id=1, replica_groups=mesh['dp'=8,'row'=2,'col'=2] {'dp','row','col'}, use_global_device_ids=true, to_apply=%region_20.21 | all-reduce | flops 4080 | bytes 32640 | tf_op jit(solution)/shard_map/psum | solution.py:265
  904.1 2.4 psum.58
  907.1 3.1 fusion.52
  910.2 94.8 %all-gather.21.cloned.1.call-done = bf16[1280,2560]{1,0:T(8,128)(2,1)} async-done(((bf16[160,2560]{1,0:T(8,128)(2,1)}), bf16[1280,2560]{1,0:T(8,128)(2,1)}) %all-gather.21.cloned.1.call-update) | async-done | bytes 6553616 | tf_op jit(solution)/shard_map/all_gather | solution.py:64
  1005.0 102.7 %all-gather.19.cloned.1.call-done = bf16[1280,2560]{1,0:T(8,128)(2,1)} async-done(((bf16[160,2560]{1,0:T(8,128)(2,1)}), bf16[1280,2560]{1,0:T(8,128)(2,1)}) %all-gather.19.cloned.1.call-update) | async-done | bytes 6553616 | tf_op jit(solution)/shard_map/all_gather | solution.py:64
  1107.7 14.4 %maximum_convert_fusion = f32[1280,2,2560]{2,0,1:T(8,128)} fusion(bf16[1280,1,2560]{2,0,1:T(8,128)(2,1)} %bitcast.86, bf16[1280,1,2560]{2,0,1:T(8,128)(2,1)} %bitcast.87), kind=kLoop, calls=%fused_computation | loop fusion | flops 13107200 | bytes 39321600 | tf_op jit(solution)/shard_map/convert_element_type | solution.py:248
  1122.1 43.6 %copy.68 = f32[1280,2,2560]{2,1,0:T(2,128)} copy(f32[1280,2,2560]{2,0,1:T(8,128)} %maximum_convert_fusion) | data formatting | bytes 52428800
  1165.7 44.9 %all-gather.23.cloned.1.call-done = bf16[2560,1280]{1,0:T(8,128)(2,1)} async-done(((bf16[320,1280]{1,0:T(8,128)(2,1)}), bf16[2560,1280]{1,0:T(8,128)(2,1)}) %all-gather.23.cloned.1.call-update) | async-done | bytes 6553616 | tf_op jit(solution)/shard_map/all_gather | solution.py:64
  1210.6 8.8 convert_element_type.112
  (267 shorter events, 47.5 us)
Async XLA Ops:
  7.2 31.7 %all-gather.9.cloned.1.call-start = ((), (), s32[]{:S(2)}) async-start(), calls=%async_computation.9 | async-start | bytes 1966080 | tf_op jit(solution)/shard_map/all_gather | solution.py:142
  11.8 52.9 %all-gather.13.cloned.1.call-start = ((), (), s32[]{:S(2)}) async-start(), calls=%async_computation.14 | async-start | bytes 1966080 | tf_op jit(solution)/shard_map/all_gather | solution.py:191
  12.5 63.1 %reduce-scatter.14.cloned.1.call-start = ((), (), s32[]{:S(2)}) async-start(), calls=%async_computation.11 | async-start | bytes 909312 | tf_op jit(solution)/shard_map/reduce_scatter | solution.py:151
  12.6 12.3 %copy-start.26 = (bf16[1280,40]{0,1:T(8,128)(2,1)S(1)}, bf16[1280,40]{0,1:T(8,128)(2,1)}, u32[]{:S(2)}) copy-start(bf16[1280,40]{0,1:T(8,128)(2,1)} %param.24) | copy-start | bytes 307204
  12.6 26.3 %copy-start.20 = (bf16[1280,256]{1,0:T(8,128)(2,1)S(1)}, bf16[1280,256]{1,0:T(8,128)(2,1)}, u32[]{:S(2)}) copy-start(bf16[1280,256]{1,0:T(8,128)(2,1)} %param.23) | copy-start | bytes 1966084
  25.1 29.0 %copy-start.15 = (bf16[1280,40]{1,0:T(8,128)(2,1)}, bf16[1280,40]{1,0:T(8,128)(2,1)S(1)}, u32[]{:S(2)}) copy-start(bf16[1280,40]{1,0:T(8,128)(2,1)S(1)} %copy.61) | copy-start | bytes 307204
  41.8 56.8 %reduce-scatter.12.cloned.1.call-start = ((), (), s32[]{:S(2)}) async-start(), calls=%async_computation.10 | async-start | bytes 15728640 | tf_op jit(solution)/shard_map/reduce_scatter | solution.py:145
  54.2 82.6 %reduce-scatter.18.cloned.1.call-start = ((), (), s32[]{:S(2)}) async-start(), calls=%async_computation.15 | async-start | bytes 7864320 | tf_op jit(solution)/shard_map/reduce_scatter | solution.py:193
  74.0 5.9 copy-start.55
  74.0 136.6 %all-gather.17.cloned.1.call-start = ((), (), s32[]{:S(2)}) async-start(), calls=%async_computation.17 | async-start | bytes 3932160 | tf_op jit(solution)/shard_map/all_gather | solution.py:217
  75.1 25.6 %copy-start.65 = (f32[40]{0:T(128)}, f32[40]{0:T(128)S(1)}, u32[]{:S(2)}) copy-start(f32[40]{0:T(128)S(1)} %exponential_negate_fusion) | copy-start | bytes 484
  75.1 25.6 %copy-start.51 = (pred[256]{0:T(512)(128)(4,1)}, pred[256]{0:T(512)(128)(4,1)S(1)}, u32[]{:S(2)}) copy-start(pred[256]{0:T(512)(128)(4,1)S(1)} %get-tuple-element.146) | copy-start | bytes 772
  75.1 79.1 %copy-start.53 = (f32[256]{0:T(256)}, f32[256]{0:T(256)S(1)}, u32[]{:S(2)}) copy-start(f32[256]{0:T(256)S(1)} %get-tuple-element.145) | copy-start | bytes 3076
  75.2 94.0 %copy-start.37 = (f32[256]{0:T(256)}, f32[256]{0:T(256)S(1)}, u32[]{:S(2)}) copy-start(f32[256]{0:T(256)S(1)} %get-tuple-element.142) | copy-start | bytes 3076
  75.2 98.1 %copy-start.33 = (f32[256]{0:T(256)}, f32[256]{0:T(256)S(1)}, u32[]{:S(2)}) copy-start(f32[256]{0:T(256)S(1)} %get-tuple-element.140) | copy-start | bytes 3076
  75.2 98.1 %copy-start.35 = (f32[256]{0:T(256)}, f32[256]{0:T(256)S(1)}, u32[]{:S(2)}) copy-start(f32[256]{0:T(256)S(1)} %get-tuple-element.141) | copy-start | bytes 3076
  75.3 25.5 %copy-start.42 = (f32[1,256]{1,0:T(1,128)}, f32[1,256]{1,0:T(1,128)S(1)}, u32[]{:S(2)}) copy-start(f32[1,256]{1,0:T(1,128)S(1)} %get-tuple-element.135) | copy-start | bytes 3076
  75.3 25.5 %copy-start.44 = (f32[1,256]{1,0:T(1,128)}, f32[1,256]{1,0:T(1,128)S(1)}, u32[]{:S(2)}) copy-start(f32[1,256]{1,0:T(1,128)S(1)} %get-tuple-element.136) | copy-start | bytes 3076
  75.3 25.5 %copy-start.46 = (f32[1,256]{1,0:T(1,128)}, f32[1,256]{1,0:T(1,128)S(1)}, u32[]{:S(2)}) copy-start(f32[1,256]{1,0:T(1,128)S(1)} %get-tuple-element.134) | copy-start | bytes 3076
  75.3 25.5 %copy-start.48 = (f32[1,256]{1,0:T(1,128)}, f32[1,256]{1,0:T(1,128)S(1)}, u32[]{:S(2)}) copy-start(f32[1,256]{1,0:T(1,128)S(1)} %get-tuple-element.133) | copy-start | bytes 3076
  79.6 74.6 %copy-start.31 = (f32[256,40]{0,1:T(8,128)}, f32[256,40]{0,1:T(8,128)S(1)}, u32[]{:S(2)}) copy-start(f32[256,40]{0,1:T(8,128)S(1)} %compare_select_fusion.2) | copy-start | bytes 122884
  79.9 74.4 %copy-start.66 = (f32[256,40]{0,1:T(8,128)}, f32[256,40]{0,1:T(8,128)S(1)}, u32[]{:S(2)}) copy-start(f32[256,40]{0,1:T(8,128)S(1)} %fusion.64) | copy-start | bytes 122884
  154.2 11.6 copy-start.11
  180.9 37.0 %all-gather.15.cloned.1.call-start = ((), (), s32[]{:S(2)}) async-start(), calls=%async_computation.16 | async-start | bytes 3932160 | tf_op jit(solution)/shard_map/all_gather | solution.py:210
  181.7 20.4 %copy-start.8 = (f32[256,296]{0,1:T(8,128)S(1)}, f32[256,296]{0,1:T(8,128)}, u32[]{:S(2)}) copy-start(f32[256,296]{0,1:T(8,128)} %reduce-scatter.14.cloned.1.call-done) | copy-start | bytes 909316
  181.7 44.2 %all-gather.11.cloned.1.call-start = ((), (), s32[]{:S(2)}) async-start(), calls=%async_computation.12 | async-start | bytes 3932160 | tf_op jit(solution)/shard_map/all_gather | solution.py:182
  182.7 18.6 %copy-start.23 = (f32[256,256]{0,1:T(8,128)S(1)}, f32[256,256]{0,1:T(8,128)}, u32[]{:S(2)}) copy-start(f32[256,256]{0,1:T(8,128)} %copy-done.22) | copy-start | bytes 786436
  182.7 18.6 %copy-start.52 = (pred[256]{0:T(512)(128)(4,1)S(1)}, pred[256]{0:T(512)(128)(4,1)}, u32[]{:S(2)}) copy-start(pred[256]{0:T(512)(128)(4,1)} %copy-done.51) | copy-start | bytes 772
  202.0 89.6 %reduce-scatter.28.cloned.1.call-start = ((), (), s32[]{:S(2)}) async-start(), calls=%async_computation.27 | async-start | bytes 1105920
  210.5 205.8 %reduce-scatter.24.cloned.1.call-start = ((), (), s32[]{:S(2)}) async-start(), calls=%async_computation.21 | async-start | bytes 7372800 | tf_op jit(solution)/shard_map/reduce_scatter | solution.py:59
  217.9 323.3 %reduce-scatter.22.cloned.1.call-start = ((), (), s32[]{:S(2)}) async-start(), calls=%async_computation.19 | async-start | bytes 7372800 | tf_op jit(solution)/shard_map/reduce_scatter | solution.py:59
  225.6 439.9 %reduce-scatter.26.cloned.1.call-start = ((), (), s32[]{:S(2)}) async-start(), calls=%async_computation.24 | async-start | bytes 7372800 | tf_op jit(solution)/shard_map/reduce_scatter | solution.py:59
  235.0 558.5 %all-reduce.32.cloned.1.call-start = ((), (), s32[]{:S(2)}) async-start(), calls=%async_computation.26 | async-start | bytes 327680 | tf_op jit(solution)/shard_map/psum | solution.py:265
  236.6 583.1 %all-reduce.30.cloned.1.call-start = ((), (), s32[]{:S(2)}) async-start(), calls=%async_computation.23 | async-start | bytes 262144 | tf_op jit(solution)/shard_map/psum | solution.py:62
  293.4 13.9 %copy-start.16 = (bf16[1280,40]{1,0:T(8,128)(2,1)S(1)}, bf16[1280,40]{1,0:T(8,128)(2,1)}, u32[]{:S(2)}) copy-start(bf16[1280,40]{1,0:T(8,128)(2,1)} %copy-done.15) | copy-start | bytes 307204
  293.4 13.9 %copy-start.21 = (bf16[1280,256]{1,0:T(8,128)(2,1)S(1)}, bf16[1280,256]{1,0:T(8,128)(2,1)}, u32[]{:S(2)}) copy-start(bf16[1280,256]{1,0:T(8,128)(2,1)} %param.23) | copy-start | bytes 1966084
  293.4 566.7 %reduce-scatter.20.cloned.1.call-start = ((), (), s32[]{:S(2)}) async-start(), calls=%async_computation.18 | async-start | bytes 3932160 | tf_op jit(solution)/shard_map/reduce_scatter | solution.py:219
  311.5 595.6 %reduce-scatter.16.cloned.1.call-start = ((), (), s32[]{:S(2)}) async-start(), calls=%async_computation.13 | async-start | bytes 3932160 | tf_op jit(solution)/shard_map/reduce_scatter | solution.py:184
  321.1 344.6 %copy-start.63 = (f32[40]{0:T(128)S(1)}, f32[40]{0:T(128)}, u32[]{:S(2)}) copy-start(f32[40]{0:T(128)} %param.30) | copy-start | bytes 484
  321.1 475.5 %slice-start.2 = ((bf16[160,296]{1,0:T(8,128)(2,1)}), bf16[160,40]{1,0:T(8,128)(2,1)S(1)}, s32[]{:S(2)}) async-start(bf16[160,296]{1,0:T(8,128)(2,1)} %reduce-scatter.28.cloned.1.call-done), calls=%async_computation.30 | async-start | bytes 81920 | tf_op jit(solution)/shard_map/slice | solution.py:63
  321.2 683.9 %all-gather.21.cloned.1.call-start = ((), (), s32[]{:S(2)}) async-start(), calls=%async_computation.22 | async-start | bytes 7372800 | tf_op jit(solution)/shard_map/all_gather | solution.py:64
  416.4 691.4 %all-gather.19.cloned.1.call-start = ((), (), s32[]{:S(2)}) async-start(), calls=%async_computation.20 | async-start | bytes 7372800 | tf_op jit(solution)/shard_map/all_gather | solution.py:64
  541.2 669.3 %all-gather.23.cloned.1.call-start = ((), (), s32[]{:S(2)}) async-start(), calls=%async_computation.25 | async-start | bytes 7372800 | tf_op jit(solution)/shard_map/all_gather | solution.py:64
  853.8 6.3 copy-start.7
  853.8 6.3 copy-start.25
  853.8 6.3 copy-start.40
  855.1 52.0 %copy-start.12 = (bf16[256,1280]{1,0:T(8,128)(2,1)S(1)}, bf16[256,1280]{1,0:T(8,128)(2,1)}, u32[]{:S(2)}) copy-start(bf16[256,1280]{1,0:T(8,128)(2,1)} %param.18) | copy-start | bytes 1966084
  860.1 47.0 %copy-start.9 = (f32[256,1280]{1,0:T(8,128)S(1)}, f32[256,1280]{1,0:T(8,128)}, u32[]{:S(2)}) copy-start(f32[256,1280]{1,0:T(8,128)} %reduce-scatter.20.cloned.1.call-done) | copy-start | bytes 3932164
  (41 other events, 103.8 us)
Sparse Core Ops, SparseCore 0:
  11.9 26.9 all-gather.8
  40.4 24.2 all-gather.12
  67.6 8.0 reduce-scatter.13
  78.4 20.1 reduce-scatter.11
  100.8 14.4 reduce-scatter.17
  181.1 12.5 all-gather.16
  195.9 12.6 all-gather.14
  210.8 12.5 all-gather.10
  227.1 64.4 reduce-scatter.27
  295.7 120.6 reduce-scatter.23
  420.4 120.7 reduce-scatter.21
  544.7 120.7 reduce-scatter.25
  672.5 120.9 all-reduce.31
  796.3 23.4 all-reduce.29
  822.5 37.5 reduce-scatter.19
  862.2 38.2 reduce-scatter.15
  902.8 102.1 all-gather.20
  1007.3 100.3 all-gather.18
  1110.1 100.3 all-gather.22
where the time goes:
time: 1230 us
  waiting for transfers between devices  837 us (68%)
  matrix products  124 us (10%)
  local copies, waits for them, and re-layouts  92.5 us (8%)
  blocking collectives  87.9 us (7%)
  other arithmetic  67.7 us (6%)
  between operations  15.3 us (1%)
    reduce_scatter x3, waiting for transfers between devices, sum_rows_over_dp(): lax.psum_scatter(part.astype(jnp.bfloat16), 'dp', scatter_dimension=0, ti...  344 us
    all_gather x3, waiting for transfers between devices, sum_rows_over_dp(): return lax.all_gather(piece, 'dp', axis=0, tiled=True)  242 us
    psum x1, waiting for transfers between devices, per_device(): lax.psum((gain_slot, head_slot, chan_slot, shared_stack), ('dp', 'row', '...  128 us
    unnamed x145, local copies, waits for them, and re-layouts  68.9 us
    unnamed x20, waiting for transfers between devices  56.6 us
    dot_general x3, matrix products, mix_bucket(): within = jnp.einsum('tsh,shp->thp', weights, values, precision=PRECISE)  45.7 us
    psum x1, blocking collectives, per_device(): lax.psum((gain_slot, head_slot, chan_slot, shared_stack), ('dp', 'row', '...  40.3 us
    all_gather x1, blocking collectives, sum_rows_over_dp(): return lax.all_gather(piece, 'dp', axis=0, tiled=True)  33 us
  transfers between devices with their start and end apart: 19, of which 14 were waited for; matrix products, arithmetic and copies ran while one was open for 18% of the time, Pallas kernels for 0%

commit v1 on v0

--- a/solution.py
+++ b/solution.py
@@ -8,6 +8,22 @@
 CAP = 256
 EPSILON = 1e-05
 PRECISE = lax.Precision.HIGHEST
+
+
+def ring_gather(x, axis, dim):
+    ways, here, step = (lax.axis_size(axis), lax.axis_index(axis), x.shape[dim])
+    shape = [n * ways if d == dim else n for d, n in enumerate(x.shape)]
+    full = lax.dynamic_update_slice_in_dim(jnp.zeros(shape, x.dtype), x, here * step, axis=dim)
+    going_up = going_down = x
+    for far in range(1, ways // 2 + 1):
+        going_up = lax.ppermute(going_up, axis, [(d, (d + 1) % ways) for d in range(ways)])
+        full = lax.dynamic_update_slice_in_dim(full, going_up, (here - far) % ways * step, axis=dim)
+        if 2 * far < ways:
+            going_down = lax.ppermute(going_down, axis, [(d, (d - 1) % ways) for d in range(ways)])
+            full = lax.dynamic_update_slice_in_dim(
+                full, going_down, (here + far) % ways * step, axis=dim
+            )
+    return full
 
 
 def layout(seq_lengths, seq_owner, bucket, capacity):
@@ -61,7 +77,7 @@
         own = piece.shape[1] - shared_cols
         tail = lax.psum(piece[:, own:].astype(jnp.float32), "col").astype(jnp.bfloat16)
         piece = jnp.concatenate([piece[:, :own], tail], axis=1)
-    return lax.all_gather(piece, "dp", axis=0, tiled=True)
+    return ring_gather(piece, "dp", 0)
 
 
 def mixer_local(

time: 1230 us -> 1320 us (1.073)
  starting transfers between devices: 1.53 us -> 59.8 us
  local copies, waits for them, and re-layouts: 92.5 us -> 126 us
  blocking collectives: 87.9 us -> 55 us
  other arithmetic: 67.7 us -> 95.6 us
    all_gather x3 -> x0, waiting for transfers between devices: 242 us -> none  [sum_rows_over_dp(): return lax.all_gather(piece, 'dp', axis=0, tiled=True)]
    ppermute x0 -> x28, waiting for transfers between devices: none -> 242 us  [the longest x16 123 us: ring_gather(): lax.ppermute(going_up, axis, [(d, (d + 1) % ways) for d in range(ways)])]
    dynamic_update_slice x0 -> x32, local copies, waits for them, and re-layouts: none -> 59.8 us  [the longest x16 30 us: ring_gather(): lax.dynamic_update_slice_in_dim(full, going_up, (here - far) % ways * ste...]
    ppermute x0 -> x28, starting transfers between devices: none -> 58.8 us  [the longest x12 42.1 us: ring_gather(): lax.ppermute(going_down, axis, [(d, (d - 1) % ways) for d in range(ways)])]
    unnamed x145 -> x158, local copies, waits for them, and re-layouts: 68.9 us -> 25 us
    psum x1, waiting for transfers between devices: 128 us -> 88.5 us  [per_device(): lax.psum((gain_slot, head_slot, chan_slot, shared_stack), ('dp', 'row', '...]
    all_gather x1 -> x0, blocking collectives: 33 us -> none  [sum_rows_over_dp(): return lax.all_gather(piece, 'dp', axis=0, tiled=True)]
    reduce_scatter x3, waiting for transfers between devices: 344 us -> 375 us  [sum_rows_over_dp(): lax.psum_scatter(part.astype(jnp.bfloat16), 'dp', scatter_dimension=0, ti...]
  transfers between devices with their start and end apart: 19 -> 44, of which waited for: 14 -> 27; matrix products, arithmetic and copies ran while one was open for 18% -> 18% of each run, Pallas kernels for 0% -> 0%
where the time goes in v1:
time: 1320 us; the launch traced here: 1310 us
  waiting for transfers between devices  841 us (64%)
  local copies, waits for them, and re-layouts  126 us (10%)
  matrix products  119 us (9%)
  other arithmetic  95.6 us (7%)
  starting transfers between devices  59.8 us (5%)
  blocking collectives  55 us (4%)
  between operations  15.6 us (1%)
    reduce_scatter x3, waiting for transfers between devices, sum_rows_over_dp(): lax.psum_scatter(part.astype(jnp.bfloat16), 'dp', scatter_dimension=0, ti...  375 us
    ppermute x16, waiting for transfers between devices, ring_gather(): lax.ppermute(going_up, axis, [(d, (d + 1) % ways) for d in range(ways)])  123 us
    ppermute x12, waiting for transfers between devices, ring_gather(): lax.ppermute(going_down, axis, [(d, (d - 1) % ways) for d in range(ways)])  118 us
    psum x1, waiting for transfers between devices, per_device(): lax.psum((gain_slot, head_slot, chan_slot, shared_stack), ('dp', 'row', '...  88.5 us
    unnamed x17, waiting for transfers between devices  56.8 us
    dot_general x3, matrix products, mix_bucket(): within = jnp.einsum('tsh,shp->thp', weights, values, precision=PRECISE)  43.7 us
    ppermute x12, starting transfers between devices, ring_gather(): lax.ppermute(going_down, axis, [(d, (d - 1) % ways) for d in range(ways)])  42.1 us
    psum x1, blocking collectives, per_device(): lax.psum((gain_slot, head_slot, chan_slot, shared_stack), ('dp', 'row', '...  40 us
  transfers between devices with their start and end apart: 44, of which 27 were waited for; matrix products, arithmetic and copies ran while one was open for 18% of the time, Pallas kernels for 0%

profile of v1, /device:TPU:0, one launch (start us, length us, event | category | flops | bytes accessed | tf_op | source)
XLA Modules:
  0.0 1311.6 jit_solution(12672848442774705218)
XLA Ops:
  12.6 12.3 copy.132
  25.1 13.7 %all-gather.6.cloned.1.call-done = bf16[512,1280]{1,0:T(8,128)(2,1)} async-done(((bf16[256,1280]{1,0:T(8,128)(2,1)}), bf16[512,1280]{1,0:T(8,128)(2,1)}) %all-gather.6.cloned.1.call-update) | async-done | bytes 1310736 | tf_op jit(solution)/shard_map/all_gather | solution.py:158
  41.8 12.3 fusion.107
  54.2 10.5 all-gather.10.cloned.1.call-done
  64.7 9.2 fusion.109
  84.7 13.9 %reduce-scatter.12.cloned.1.call-done = f32[256,5120]{1,0:T(8,128)} async-done(((f32[512,5120]{1,0:T(8,128)}), f32[256,5120]{1,0:T(8,128)}) %reduce-scatter.12.cloned.1.call-update) | async-done | bytes 5242896 | tf_op jit(solution)/shard_map/reduce_scatter | solution.py:161
  110.2 15.7 %fusion.33 = f32[256,40,64]{0,2,1:T(8,128)} fusion(f32[256,40,64]{0,2,1:T(8,128)} %bitcast.101, f32[256,40]{0,1:T(8,128)} %copy-done.33, f32[256,256]{1,0:T(8,128)} %convolution_select_fusion, f32[256,40]{0,1:T(8,128)} %fusion.64, pred[256,256]{1,0:T(8,128)(4,1)S(1)} %fusion.65, f32[256]{0:T(256)S(1)} %copy-done.55, f32[40]{0:T(128)S(1)} %copy-done.65), kind=kOutput, calls=%fused_computation.49 | convolution fusion | flops 2025717760 | bytes 5653664 | tf_op jit(solution)/shard_map/jvp(tsh,shp->thp)/dot_general | solution.py:69
  128.1 4.0 multiply_reduce_fusion.8
  132.1 4.9 psum.56
  141.5 5.1 psum.57
  146.6 6.9 multiply_reduce_fusion.1
  155.8 11.6 bitcast_add_fusion
  167.6 16.3 %fusion.8 = (f32[256,40]{0,1:T(8,128)S(1)}, f32[256,40]{0,1:T(8,128)S(1)}, f32[256,40]{0,1:T(8,128)S(1)}, f32[256,256]{1,0:T(8,128)S(1)}) fusion(f32[256,40]{0,1:T(8,128)S(1)} %copy-done.34, f32[256,256]{1,0:T(8,128)S(1)} %copy-done.69, f32[256,40]{0,1:T(8,128)S(1)} %copy-done.73, pred[256,256]{1,0:T(8,128)(4,1)S(1)} %fusion.65, ...), kind=kOutput, calls=%fused_computation.15 | convolution fusion | flops 2047903744 | bytes 6038528 | tf_op jit(solution)/shard_map/transpose(jvp(tsh,shp->thp))/dot_general | solution.py:69
  193.8 5.5 multiply_reduce_fusion.6
  215.5 54.6 %reduce-scatter.28.cloned.1.call-done = bf16[160,296]{1,0:T(8,128)(2,1)} async-done(((bf16[1280,296]{1,0:T(8,128)(2,1)}), bf16[160,296]{1,0:T(8,128)(2,1)}) %reduce-scatter.28.cloned.1.call-update) | async-done | bytes 94736
  272.7 9.9 all-gather.14.cloned.1.call-done
  282.6 14.7 %all-gather.12.cloned.1.call-done = bf16[512,2560]{1,0:T(8,128)(2,1)} async-done(((bf16[256,2560]{1,0:T(8,128)(2,1)}), bf16[512,2560]{1,0:T(8,128)(2,1)}) %all-gather.12.cloned.1.call-update) | async-done | bytes 2621456 | tf_op jit(solution)/shard_map/all_gather | solution.py:226
  297.3 12.7 fusion.9
  313.7 8.7 fusion.108
  323.8 7.3 convolution_convert_fusion.1
  331.2 7.3 convolution_convert_fusion.2
  340.2 6.8 convolution_convert_fusion
  353.8 4.4 collective-permute-done.14
  368.9 4.2 collective-permute-start.19
  376.9 88.5 %all-reduce.32.cloned.1.call-done = f32[6,2,2560]{2,0,1:T(8,128)} async-done(((f32[6,2,2560]{2,0,1:T(8,128)}), f32[6,2,2560]{2,0,1:T(8,128)}) %all-reduce.32.cloned.1.call-update) | async-done | bytes 122896 | tf_op jit(solution)/shard_map/psum | solution.py:281
  491.5 15.7 %reduce-scatter.20.cloned.1.call-done = f32[256,1280]{1,0:T(8,128)} async-done(((f32[512,1280]{1,0:T(8,128)}), f32[256,1280]{1,0:T(8,128)}) %reduce-scatter.20.cloned.1.call-update) | async-done | bytes 1310736 | tf_op jit(solution)/shard_map/reduce_scatter | solution.py:235
  509.1 40.0 %all-reduce.26 = (f32[2,1280]{1,0:T(2,128)S(1)}, f32[5,256]{1,0:T(8,128)S(1)}, f32[3,2,40]{2,1,0:T(2,128)S(1)}) all-reduce(f32[2,1280]{1,0:T(2,128)S(1)} %broadcast_multiply_fusion.7, f32[5,256]{1,0:T(8,128)S(1)} %pad_maximum_fusion.6, ...), channel_id=1, replica_groups=mesh['dp'=8,'row'=2,'col'=2] {'dp','row','col'}, use_global_device_ids=true, to_apply=%region_20.21 | all-reduce | flops 4080 | bytes 32640 | tf_op jit(solution)/shard_map/psum | solution.py:281
  557.2 116.3 %reduce-scatter.24.cloned.1.call-done = bf16[160,2560]{1,0:T(8,128)(2,1)} async-done(((bf16[1280,2560]{1,0:T(8,128)(2,1)}), bf16[160,2560]{1,0:T(8,128)(2,1)}) %reduce-scatter.24.cloned.1.call-update) | async-done | bytes 819216 | tf_op jit(solution)/shard_map/reduce_scatter | solution.py:75
  678.3 134.7 %reduce-scatter.22.cloned.1.call-done = bf16[160,2560]{1,0:T(8,128)(2,1)} async-done(((bf16[1280,2560]{1,0:T(8,128)(2,1)}), bf16[160,2560]{1,0:T(8,128)(2,1)}) %reduce-scatter.22.cloned.1.call-update) | async-done | bytes 819216 | tf_op jit(solution)/shard_map/reduce_scatter | solution.py:75
  817.7 8.1 stack.49.clone
  828.3 124.2 %reduce-scatter.26.cloned.1.call-done = bf16[320,1280]{1,0:T(8,128)(2,1)} async-done(((bf16[2560,1280]{1,0:T(8,128)(2,1)}), bf16[320,1280]{1,0:T(8,128)(2,1)}) %reduce-scatter.26.cloned.1.call-update) | async-done | bytes 819216 | tf_op jit(solution)/shard_map/reduce_scatter | solution.py:75
  954.3 7.1 stack.49.clone.1
  976.3 4.7 collective-permute-start.10
  982.5 25.8 %collective-permute-done.21 = bf16[320,1280]{1,0:T(8,128)(2,1)S(1)} collective-permute-done((bf16[320,1280]{1,0:T(8,128)(2,1)}, bf16[320,1280]{1,0:T(8,128)(2,1)S(1)}, u32[]{:S(2)}, u32[]{:S(2)}) %collective-permute-start.21) | collective-permute-done | bytes 819232 | tf_op jit(solution)/shard_map/ppermute | solution.py:19
  1013.9 13.7 %collective-permute-done.22 = bf16[320,1280]{1,0:T(8,128)(2,1)S(1)} collective-permute-done((bf16[320,1280]{1,0:T(8,128)(2,1)S(1)}, bf16[320,1280]{1,0:T(8,128)(2,1)S(1)}, u32[]{:S(2)}, u32[]{:S(2)}) %collective-permute-start.22) | collective-permute-done | bytes 819232 | tf_op jit(solution)/shard_map/ppermute | solution.py:22
  1028.6 14.8 %collective-permute-done.9 = bf16[160,2560]{1,0:T(8,128)(2,1)S(1)} collective-permute-done((bf16[160,2560]{1,0:T(8,128)(2,1)}, bf16[160,2560]{1,0:T(8,128)(2,1)S(1)}, u32[]{:S(2)}, u32[]{:S(2)}) %collective-permute-start.9) | collective-permute-done | bytes 819232 | tf_op jit(solution)/shard_map/ppermute | solution.py:19
  1049.2 13.6 %collective-permute-done.10 = bf16[160,2560]{1,0:T(8,128)(2,1)S(1)} collective-permute-done((bf16[160,2560]{1,0:T(8,128)(2,1)S(1)}, bf16[160,2560]{1,0:T(8,128)(2,1)S(1)}, u32[]{:S(2)}, u32[]{:S(2)}) %collective-permute-start.10) | collective-permute-done | bytes 819232 | tf_op jit(solution)/shard_map/ppermute | solution.py:22
  1065.2 13.3 %collective-permute-done.2 = bf16[160,2560]{1,0:T(8,128)(2,1)S(1)} collective-permute-done((bf16[160,2560]{1,0:T(8,128)(2,1)S(1)}, bf16[160,2560]{1,0:T(8,128)(2,1)S(1)}, u32[]{:S(2)}, u32[]{:S(2)}) %collective-permute-start.2) | collective-permute-done | bytes 819232 | tf_op jit(solution)/shard_map/ppermute | solution.py:19
  1083.4 14.5 %collective-permute-done.3 = bf16[160,2560]{1,0:T(8,128)(2,1)S(1)} collective-permute-done((bf16[160,2560]{1,0:T(8,128)(2,1)S(1)}, bf16[160,2560]{1,0:T(8,128)(2,1)S(1)}, u32[]{:S(2)}, u32[]{:S(2)}) %collective-permute-start.3) | collective-permute-done | bytes 819232 | tf_op jit(solution)/shard_map/ppermute | solution.py:22
  1097.9 15.6 %collective-permute-done.23 = bf16[320,1280]{1,0:T(8,128)(2,1)S(1)} collective-permute-done((bf16[320,1280]{1,0:T(8,128)(2,1)S(1)}, bf16[320,1280]{1,0:T(8,128)(2,1)S(1)}, u32[]{:S(2)}, u32[]{:S(2)}) %collective-permute-start.23) | collective-permute-done | bytes 819232 | tf_op jit(solution)/shard_map/ppermute | solution.py:19
  1119.3 13.7 %collective-permute-done.24 = bf16[320,1280]{1,0:T(8,128)(2,1)S(1)} collective-permute-done((bf16[320,1280]{1,0:T(8,128)(2,1)S(1)}, bf16[320,1280]{1,0:T(8,128)(2,1)S(1)}, u32[]{:S(2)}, u32[]{:S(2)}) %collective-permute-start.24) | collective-permute-done | bytes 819232 | tf_op jit(solution)/shard_map/ppermute | solution.py:22
  1133.9 14.7 %collective-permute-done.11 = bf16[160,2560]{1,0:T(8,128)(2,1)S(1)} collective-permute-done((bf16[160,2560]{1,0:T(8,128)(2,1)S(1)}, bf16[160,2560]{1,0:T(8,128)(2,1)S(1)}, u32[]{:S(2)}, u32[]{:S(2)}) %collective-permute-start.11) | collective-permute-done | bytes 819232 | tf_op jit(solution)/shard_map/ppermute | solution.py:19
  1154.6 13.5 %collective-permute-done.12 = bf16[160,2560]{1,0:T(8,128)(2,1)S(1)} collective-permute-done((bf16[160,2560]{1,0:T(8,128)(2,1)S(1)}, bf16[160,2560]{1,0:T(8,128)(2,1)S(1)}, u32[]{:S(2)}, u32[]{:S(2)}) %collective-permute-start.12) | collective-permute-done | bytes 819232 | tf_op jit(solution)/shard_map/ppermute | solution.py:22
  1168.1 15.7 %collective-permute-done.4 = bf16[160,2560]{1,0:T(8,128)(2,1)S(1)} collective-permute-done((bf16[160,2560]{1,0:T(8,128)(2,1)S(1)}, bf16[160,2560]{1,0:T(8,128)(2,1)S(1)}, u32[]{:S(2)}, u32[]{:S(2)}) %collective-permute-start.4) | collective-permute-done | bytes 819232 | tf_op jit(solution)/shard_map/ppermute | solution.py:19
  1188.8 12.6 collective-permute-done.25
  1206.4 49.4 %collective-permute-done.26 = bf16[320,1280]{1,0:T(8,128)(2,1)S(1)} collective-permute-done((bf16[320,1280]{1,0:T(8,128)(2,1)S(1)}, bf16[320,1280]{1,0:T(8,128)(2,1)S(1)}, u32[]{:S(2)}, u32[]{:S(2)}) %collective-permute-start.26) | collective-permute-done | bytes 819232 | tf_op jit(solution)/shard_map/ppermute | solution.py:22
  1259.1 8.8 convert_element_type.112
  1271.8 33.1 %maximum_convert_fusion = f32[1280,2,2560]{2,1,0:T(2,128)} fusion(bf16[1280,1,2560]{2,1,0:T(2,128)(2,1)} %copy_dynamic-update-slice_fusion, bf16[1280,1,2560]{2,1,0:T(2,128)(2,1)S(1)} %copy_dynamic-update-slice_fusion.8), kind=kLoop, calls=%fused_computation | loop fusion | flops 26214400 | bytes 39321600 | tf_op jit(solution)/shard_map/convert_element_type | solution.py:264
  (363 shorter events, 211.0 us)
Async XLA Ops:
  7.2 31.7 %all-gather.6.cloned.1.call-start = ((), (), s32[]{:S(2)}) async-start(), calls=%async_computation.9 | async-start | bytes 1966080 | tf_op jit(solution)/shard_map/all_gather | solution.py:158
  11.8 53.0 %all-gather.10.cloned.1.call-start = ((), (), s32[]{:S(2)}) async-start(), calls=%async_computation.14 | async-start | bytes 1966080 | tf_op jit(solution)/shard_map/all_gather | solution.py:207
  12.5 63.5 %reduce-scatter.14.cloned.1.call-start = ((), (), s32[]{:S(2)}) async-start(), calls=%async_computation.11 | async-start | bytes 909312 | tf_op jit(solution)/shard_map/reduce_scatter | solution.py:167
  25.1 29.0 %copy-start.17 = (bf16[1280,40]{1,0:T(8,128)(2,1)}, bf16[1280,40]{1,0:T(8,128)(2,1)S(1)}, u32[]{:S(2)}) copy-start(bf16[1280,40]{1,0:T(8,128)(2,1)S(1)} %copy.105) | copy-start | bytes 307204
  41.8 56.8 %reduce-scatter.12.cloned.1.call-start = ((), (), s32[]{:S(2)}) async-start(), calls=%async_computation.10 | async-start | bytes 15728640 | tf_op jit(solution)/shard_map/reduce_scatter | solution.py:161
  54.2 83.4 %reduce-scatter.18.cloned.1.call-start = ((), (), s32[]{:S(2)}) async-start(), calls=%async_computation.15 | async-start | bytes 7864320 | tf_op jit(solution)/shard_map/reduce_scatter | solution.py:209
  74.0 196.0 %reduce-scatter.28.cloned.1.call-start = ((), (), s32[]{:S(2)}) async-start(), calls=%async_computation.24 | async-start | bytes 1105920
  205.3 77.2 %all-gather.14.cloned.1.call-start = ((), (), s32[]{:S(2)}) async-start(), calls=%async_computation.17 | async-start | bytes 3932160 | tf_op jit(solution)/shard_map/all_gather | solution.py:233
  213.7 83.5 %all-gather.12.cloned.1.call-start = ((), (), s32[]{:S(2)}) async-start(), calls=%async_computation.16 | async-start | bytes 3932160 | tf_op jit(solution)/shard_map/all_gather | solution.py:226
  214.5 99.2 %all-gather.8.cloned.1.call-start = ((), (), s32[]{:S(2)}) async-start(), calls=%async_computation.12 | async-start | bytes 3932160 | tf_op jit(solution)/shard_map/all_gather | solution.py:198
  215.2 132.8 %all-reduce.30.cloned.1.call-start = ((), (), s32[]{:S(2)}) async-start(), calls=%async_computation.21 | async-start | bytes 262144 | tf_op jit(solution)/shard_map/psum | solution.py:78
  271.8 193.6 %all-reduce.32.cloned.1.call-start = ((), (), s32[]{:S(2)}) async-start(), calls=%async_computation.23 | async-start | bytes 327680 | tf_op jit(solution)/shard_map/psum | solution.py:281
  272.6 37.3 %copy-start.15 = (bf16[512,296]{0,1:T(8,128)(2,1)S(1)}, bf16[512,296]{0,1:T(8,128)(2,1)}, u32[]{:S(2)}) copy-start(bf16[512,296]{0,1:T(8,128)(2,1)} %copy-done.14) | copy-start | bytes 909316
  272.7 37.3 %copy-start.18 = (bf16[1280,40]{1,0:T(8,128)(2,1)S(1)}, bf16[1280,40]{1,0:T(8,128)(2,1)}, u32[]{:S(2)}) copy-start(bf16[1280,40]{1,0:T(8,128)(2,1)} %copy-done.17) | copy-start | bytes 307204
  272.7 234.5 %reduce-scatter.20.cloned.1.call-start = ((), (), s32[]{:S(2)}) async-start(), calls=%async_computation.18 | async-start | bytes 3932160 | tf_op jit(solution)/shard_map/reduce_scatter | solution.py:235
  313.5 240.4 %reduce-scatter.16.cloned.1.call-start = ((), (), s32[]{:S(2)}) async-start(), calls=%async_computation.13 | async-start | bytes 3932160 | tf_op jit(solution)/shard_map/reduce_scatter | solution.py:200
  322.5 351.0 %reduce-scatter.24.cloned.1.call-start = ((), (), s32[]{:S(2)}) async-start(), calls=%async_computation.20 | async-start | bytes 7372800 | tf_op jit(solution)/shard_map/reduce_scatter | solution.py:75
  331.1 481.8 %reduce-scatter.22.cloned.1.call-start = ((), (), s32[]{:S(2)}) async-start(), calls=%async_computation.19 | async-start | bytes 7372800 | tf_op jit(solution)/shard_map/reduce_scatter | solution.py:75
  338.5 613.9 %reduce-scatter.26.cloned.1.call-start = ((), (), s32[]{:S(2)}) async-start(), calls=%async_computation.22 | async-start | bytes 7372800 | tf_op jit(solution)/shard_map/reduce_scatter | solution.py:75
  348.9 9.2 collective-permute-start.14
  350.8 9.6 collective-permute-start.15
  358.1 8.7 collective-permute-start.16
  360.3 8.6 collective-permute-start.17
  366.8 9.5 collective-permute-start.18
  368.9 115.2 %collective-permute-start.19 = (bf16[160,296]{0,1:T(8,128)(2,1)S(1)}, bf16[160,296]{0,1:T(8,128)(2,1)S(1)}, u32[]{:S(2)}, u32[]{:S(2)}) collective-permute-start(bf16[160,296]{0,1:T(8,128)(2,1)S(1)} %collective-permute-done.17), channel_id=1, source_target_pairs={{0,28},{4,0},{8,4},{12,8},{16,12},{20,16},{24,20},{28,24},{1,29},{... | collective-permute-start | bytes 284168 | tf_op jit(solution)/shard_map/ppermute | solution.py:22
  376.3 110.7 %collective-permute-start.20 = (bf16[160,296]{0,1:T(8,128)(2,1)S(1)}, bf16[160,296]{0,1:T(8,128)(2,1)S(1)}, u32[]{:S(2)}, u32[]{:S(2)}) collective-permute-start(bf16[160,296]{0,1:T(8,128)(2,1)S(1)} %collective-permute-done.18), channel_id=1, source_target_pairs={{0,4},{4,8},{8,12},{12,16},{16,20},{20,24},{24,28},{28,0},{1,5},{5... | collective-permute-start | bytes 284168 | tf_op jit(solution)/shard_map/ppermute | solution.py:19
  507.1 46.8 %copy-start.12 = (f32[256,1280]{1,0:T(8,128)S(1)}, f32[256,1280]{1,0:T(8,128)}, u32[]{:S(2)}) copy-start(f32[256,1280]{1,0:T(8,128)} %reduce-scatter.20.cloned.1.call-done) | copy-start | bytes 3932164
  673.5 293.4 %collective-permute-start.7 = (bf16[160,2560]{1,0:T(8,128)(2,1)}, bf16[160,2560]{1,0:T(8,128)(2,1)}, u32[]{:S(2)}, u32[]{:S(2)}) collective-permute-start(bf16[160,2560]{1,0:T(8,128)(2,1)} %reduce-scatter.24.cloned.1.call-done), channel_id=1, source_target_pairs={{0,4},{4,8},{8,12},{12,16},{16,20},{20,24},{24,28},{28,0},{1,5},{5... | collective-permute-start | bytes 2457608 | tf_op jit(solution)/shard_map/ppermute | solution.py:19
  675.0 298.8 %collective-permute-start.8 = (bf16[160,2560]{1,0:T(8,128)(2,1)}, bf16[160,2560]{1,0:T(8,128)(2,1)S(1)}, u32[]{:S(2)}, u32[]{:S(2)}) collective-permute-start(bf16[160,2560]{1,0:T(8,128)(2,1)} %reduce-scatter.24.cloned.1.call-done), channel_id=1, source_target_pairs={{0,28},{4,0},{8,4},{12,8},{16,12},{20,16},{24,20},{28,24},{1,29},{... | collective-permute-start | bytes 2457608 | tf_op jit(solution)/shard_map/ppermute | solution.py:22
  813.0 163.3 %collective-permute-start = (bf16[160,2560]{1,0:T(8,128)(2,1)}, bf16[160,2560]{1,0:T(8,128)(2,1)S(1)}, u32[]{:S(2)}, u32[]{:S(2)}) collective-permute-start(bf16[160,2560]{1,0:T(8,128)(2,1)} %reduce-scatter.22.cloned.1.call-done), channel_id=1, source_target_pairs={{0,4},{4,8},{8,12},{12,16},{16,20},{20,24},{24,28},{28,0},{1,5},{5... | collective-permute-start | bytes 2457608 | tf_op jit(solution)/shard_map/ppermute | solution.py:19
  814.4 168.0 %collective-permute-start.1 = (bf16[160,2560]{1,0:T(8,128)(2,1)}, bf16[160,2560]{1,0:T(8,128)(2,1)S(1)}, u32[]{:S(2)}, u32[]{:S(2)}) collective-permute-start(bf16[160,2560]{1,0:T(8,128)(2,1)} %reduce-scatter.22.cloned.1.call-done), channel_id=1, source_target_pairs={{0,28},{4,0},{8,4},{12,8},{16,12},{20,16},{24,20},{28,24},{1,29},{... | collective-permute-start | bytes 2457608 | tf_op jit(solution)/shard_map/ppermute | solution.py:22
  952.4 55.9 %collective-permute-start.21 = (bf16[320,1280]{1,0:T(8,128)(2,1)}, bf16[320,1280]{1,0:T(8,128)(2,1)S(1)}, u32[]{:S(2)}, u32[]{:S(2)}) collective-permute-start(bf16[320,1280]{1,0:T(8,128)(2,1)} %reduce-scatter.26.cloned.1.call-done), channel_id=1, source_target_pairs={{0,4},{4,8},{8,12},{12,16},{16,20},{20,24},{24,28},{28,0},{1,5},{5... | collective-permute-start | bytes 2457608 | tf_op jit(solution)/shard_map/ppermute | solution.py:19
  967.0 60.7 %collective-permute-start.22 = (bf16[320,1280]{1,0:T(8,128)(2,1)S(1)}, bf16[320,1280]{1,0:T(8,128)(2,1)S(1)}, u32[]{:S(2)}, u32[]{:S(2)}) collective-permute-start(bf16[320,1280]{1,0:T(8,128)(2,1)S(1)} %copy-done.23), channel_id=1, source_target_pairs={{0,28},{4,0},{8,4},{12,8},{16,12},{20,16},{24,20},{28,24},{1,29},{... | collective-permute-start | bytes 2457608 | tf_op jit(solution)/shard_map/ppermute | solution.py:22
  976.3 67.1 %collective-permute-start.9 = (bf16[160,2560]{1,0:T(8,128)(2,1)}, bf16[160,2560]{1,0:T(8,128)(2,1)S(1)}, u32[]{:S(2)}, u32[]{:S(2)}) collective-permute-start(bf16[160,2560]{1,0:T(8,128)(2,1)} %collective-permute-done.7), channel_id=1, source_target_pairs={{0,4},{4,8},{8,12},{12,16},{16,20},{20,24},{24,28},{28,0},{1,5},{5... | collective-permute-start | bytes 2457608 | tf_op jit(solution)/shard_map/ppermute | solution.py:19
  976.3 86.5 %collective-permute-start.10 = (bf16[160,2560]{1,0:T(8,128)(2,1)S(1)}, bf16[160,2560]{1,0:T(8,128)(2,1)S(1)}, u32[]{:S(2)}, u32[]{:S(2)}) collective-permute-start(bf16[160,2560]{1,0:T(8,128)(2,1)S(1)} %collective-permute-done.8), channel_id=1, source_target_pairs={{0,28},{4,0},{8,4},{12,8},{16,12},{20,16},{24,20},{28,24},{1,29},{... | collective-permute-start | bytes 2457608 | tf_op jit(solution)/shard_map/ppermute | solution.py:22
  982.4 96.1 %collective-permute-start.2 = (bf16[160,2560]{1,0:T(8,128)(2,1)S(1)}, bf16[160,2560]{1,0:T(8,128)(2,1)S(1)}, u32[]{:S(2)}, u32[]{:S(2)}) collective-permute-start(bf16[160,2560]{1,0:T(8,128)(2,1)S(1)} %collective-permute-done), channel_id=1, source_target_pairs={{0,4},{4,8},{8,12},{12,16},{16,20},{20,24},{24,28},{28,0},{1,5},{5... | collective-permute-start | bytes 2457608 | tf_op jit(solution)/shard_map/ppermute | solution.py:19
  1008.3 89.6 %collective-permute-start.3 = (bf16[160,2560]{1,0:T(8,128)(2,1)S(1)}, bf16[160,2560]{1,0:T(8,128)(2,1)S(1)}, u32[]{:S(2)}, u32[]{:S(2)}) collective-permute-start(bf16[160,2560]{1,0:T(8,128)(2,1)S(1)} %collective-permute-done.1), channel_id=1, source_target_pairs={{0,28},{4,0},{8,4},{12,8},{16,12},{20,16},{24,20},{28,24},{1,29},{... | collective-permute-start | bytes 2457608 | tf_op jit(solution)/shard_map/ppermute | solution.py:22
  1027.7 85.8 %collective-permute-start.23 = (bf16[320,1280]{1,0:T(8,128)(2,1)S(1)}, bf16[320,1280]{1,0:T(8,128)(2,1)S(1)}, u32[]{:S(2)}, u32[]{:S(2)}) collective-permute-start(bf16[320,1280]{1,0:T(8,128)(2,1)S(1)} %collective-permute-done.21), channel_id=1, source_target_pairs={{0,4},{4,8},{8,12},{12,16},{16,20},{20,24},{24,28},{28,0},{1,5},{5... | collective-permute-start | bytes 2457608 | tf_op jit(solution)/shard_map/ppermute | solution.py:19
  1043.4 89.6 %collective-permute-start.24 = (bf16[320,1280]{1,0:T(8,128)(2,1)S(1)}, bf16[320,1280]{1,0:T(8,128)(2,1)S(1)}, u32[]{:S(2)}, u32[]{:S(2)}) collective-permute-start(bf16[320,1280]{1,0:T(8,128)(2,1)S(1)} %collective-permute-done.22), channel_id=1, source_target_pairs={{0,28},{4,0},{8,4},{12,8},{16,12},{20,16},{24,20},{28,24},{1,29},{... | collective-permute-start | bytes 2457608 | tf_op jit(solution)/shard_map/ppermute | solution.py:22
  1065.2 83.4 %collective-permute-start.11 = (bf16[160,2560]{1,0:T(8,128)(2,1)S(1)}, bf16[160,2560]{1,0:T(8,128)(2,1)S(1)}, u32[]{:S(2)}, u32[]{:S(2)}) collective-permute-start(bf16[160,2560]{1,0:T(8,128)(2,1)S(1)} %collective-permute-done.9), channel_id=1, source_target_pairs={{0,4},{4,8},{8,12},{12,16},{16,20},{20,24},{24,28},{28,0},{1,5},{5... | collective-permute-start | bytes 2457608 | tf_op jit(solution)/shard_map/ppermute | solution.py:19
  1078.5 89.6 %collective-permute-start.12 = (bf16[160,2560]{1,0:T(8,128)(2,1)S(1)}, bf16[160,2560]{1,0:T(8,128)(2,1)S(1)}, u32[]{:S(2)}, u32[]{:S(2)}) collective-permute-start(bf16[160,2560]{1,0:T(8,128)(2,1)S(1)} %collective-permute-done.10), channel_id=1, source_target_pairs={{0,28},{4,0},{8,4},{12,8},{16,12},{20,16},{24,20},{28,24},{1,29},{... | collective-permute-start | bytes 2457608 | tf_op jit(solution)/shard_map/ppermute | solution.py:22
  1097.9 86.0 %collective-permute-start.4 = (bf16[160,2560]{1,0:T(8,128)(2,1)S(1)}, bf16[160,2560]{1,0:T(8,128)(2,1)S(1)}, u32[]{:S(2)}, u32[]{:S(2)}) collective-permute-start(bf16[160,2560]{1,0:T(8,128)(2,1)S(1)} %collective-permute-done.2), channel_id=1, source_target_pairs={{0,4},{4,8},{8,12},{12,16},{16,20},{20,24},{24,28},{28,0},{1,5},{5... | collective-permute-start | bytes 2457608 | tf_op jit(solution)/shard_map/ppermute | solution.py:19
  1113.5 143.2 %collective-permute-start.5 = (bf16[160,2560]{1,0:T(8,128)(2,1)S(1)}, bf16[160,2560]{1,0:T(8,128)(2,1)S(1)}, u32[]{:S(2)}, u32[]{:S(2)}) collective-permute-start(bf16[160,2560]{1,0:T(8,128)(2,1)S(1)} %collective-permute-done.3), channel_id=1, source_target_pairs={{0,28},{4,0},{8,4},{12,8},{16,12},{20,16},{24,20},{28,24},{1,29},{... | collective-permute-start | bytes 2457608 | tf_op jit(solution)/shard_map/ppermute | solution.py:22
  1133.0 68.4 %collective-permute-start.25 = (bf16[320,1280]{1,0:T(8,128)(2,1)S(1)}, bf16[320,1280]{1,0:T(8,128)(2,1)S(1)}, u32[]{:S(2)}, u32[]{:S(2)}) collective-permute-start(bf16[320,1280]{1,0:T(8,128)(2,1)S(1)} %collective-permute-done.23), channel_id=1, source_target_pairs={{0,4},{4,8},{8,12},{12,16},{16,20},{20,24},{24,28},{28,0},{1,5},{5... | collective-permute-start | bytes 2457608 | tf_op jit(solution)/shard_map/ppermute | solution.py:19
  1148.6 107.2 %collective-permute-start.26 = (bf16[320,1280]{1,0:T(8,128)(2,1)S(1)}, bf16[320,1280]{1,0:T(8,128)(2,1)S(1)}, u32[]{:S(2)}, u32[]{:S(2)}) collective-permute-start(bf16[320,1280]{1,0:T(8,128)(2,1)S(1)} %collective-permute-done.24), channel_id=1, source_target_pairs={{0,28},{4,0},{8,4},{12,8},{16,12},{20,16},{24,20},{28,24},{1,29},{... | collective-permute-start | bytes 2457608 | tf_op jit(solution)/shard_map/ppermute | solution.py:22
  1168.1 99.8 %collective-permute-start.13 = (bf16[160,2560]{1,0:T(8,128)(2,1)S(1)}, bf16[160,2560]{1,0:T(8,128)(2,1)S(1)}, u32[]{:S(2)}, u32[]{:S(2)}) collective-permute-start(bf16[160,2560]{1,0:T(8,128)(2,1)S(1)} %collective-permute-done.11), channel_id=1, source_target_pairs={{0,4},{4,8},{8,12},{12,16},{16,20},{20,24},{24,28},{28,0},{1,5},{5... | collective-permute-start | bytes 2457608 | tf_op jit(solution)/shard_map/ppermute | solution.py:19
  1183.8 86.5 %collective-permute-start.6 = (bf16[160,2560]{1,0:T(8,128)(2,1)S(1)}, bf16[160,2560]{1,0:T(8,128)(2,1)S(1)}, u32[]{:S(2)}, u32[]{:S(2)}) collective-permute-start(bf16[160,2560]{1,0:T(8,128)(2,1)S(1)} %collective-permute-done.4), channel_id=1, source_target_pairs={{0,4},{4,8},{8,12},{12,16},{16,20},{20,24},{24,28},{28,0},{1,5},{5... | collective-permute-start | bytes 2457608 | tf_op jit(solution)/shard_map/ppermute | solution.py:19
  1201.4 56.7 %collective-permute-start.27 = (bf16[320,1280]{1,0:T(8,128)(2,1)S(1)}, bf16[320,1280]{1,0:T(8,128)(2,1)S(1)}, u32[]{:S(2)}, u32[]{:S(2)}) collective-permute-start(bf16[320,1280]{1,0:T(8,128)(2,1)S(1)} %collective-permute-done.25), channel_id=1, source_target_pairs={{0,4},{4,8},{8,12},{12,16},{16,20},{20,24},{24,28},{28,0},{1,5},{5... | collective-permute-start | bytes 2457608 | tf_op jit(solution)/shard_map/ppermute | solution.py:19
  (75 other events, 569.8 us)
Sparse Core Ops, SparseCore 0:
  11.9 26.9 all-gather.5
  40.4 24.2 all-gather.9
  67.6 8.0 reduce-scatter.13
  78.4 20.1 reduce-scatter.11
  100.7 14.4 reduce-scatter.17
  205.5 64.5 reduce-scatter.27
  272.2 10.3 all-gather.13
  284.7 12.5 all-gather.11
  299.4 12.5 all-gather.7
  314.0 22.5 all-reduce.29
  342.8 122.5 all-reduce.31
  467.5 39.5 reduce-scatter.19
  509.5 38.2 reduce-scatter.15
  551.8 121.6 reduce-scatter.23
  678.0 134.9 reduce-scatter.21
  816.4 135.9 reduce-scatter.25
